TPU v7x, 512 devices: a whole 4x4x16 slice. The times are simulated.
512 devices in a mesh: group: 32 (over y, z_hi, core), mp: 16 (over z_lo, x).
Axes of the slice: x: 4, y: 4, z: 16 (z_hi: 4, z_lo: 4; z = z_hi * 4 + z_lo), core: 2. Of those that a mesh axis runs over, the one named last changes fastest.
Arguments:
- hidden: bfloat16 [8192, 8192], P('group', 'mp'), may hold values from -6 to 6
- targets: bfloat16 [8192, 4096], P('group', 'mp'), may hold values from -6 to 6
- counts: int32 [32, 4], P('group'), may hold values from 1 to 64, 160 in all within a row
- master: float32 [8192, 4096], P('group', 'mp'), may hold values from -3 to 3
Outputs:
- new_master: float32 [8192, 4096], P('group', 'mp')
- refreshed: bfloat16 [8192, 4096], P('group', 'mp')
Inputs may be any that keep to these rules, and one draw needn't show every extreme that they name: Each serving group's counts sum to 160; in every group one sequence has exactly 64.
All inputs are finite; a program needn't handle non-finite values.
Results may differ from a plain program's by a relative error of at most 0.024.
Values may be sent and summed in bfloat16 or wider, within the bound.
A program may use at most 64 MiB of HBM per device.

v0:
```python
import jax
import jax.numpy as jnp
from jax import lax
from jax.sharding import PartitionSpec as P


def shards(hidden, targets, counts, master):
    capacity = hidden.shape[0]
    slots = capacity // counts.shape[1]
    x_full = lax.all_gather(hidden, "mp", axis=1, tiled=True)
    width = x_full.shape[1]
    scale = width ** (-0.5)
    weights16 = master.astype(jnp.bfloat16)

    def add_rows(piece):
        return jnp.dot(x_full, piece, preferred_element_type=jnp.float32)

    pred = add_rows(lax.all_gather(weights16, "group", axis=0, tiled=True)) * scale
    valid = (jnp.arange(slots, dtype=jnp.int32)[None, :] < counts[0][:, None]).reshape(capacity)
    diff = jnp.clip(pred - targets.astype(jnp.float32), -1.0, 1.0)
    err = (diff * valid[:, None].astype(jnp.float32)).astype(jnp.bfloat16)
    own_rows = master.shape[0]
    full_part = (
        lax.dot_general(x_full, err, (((0,), (0,)), ((), ())), preferred_element_type=jnp.float32)
        * scale
    )
    summed = lax.psum(full_part.astype(jnp.bfloat16), "group").astype(jnp.float32)
    square_sum = lax.psum(jnp.sum(summed * summed), "mp")
    grad = lax.dynamic_slice_in_dim(summed, lax.axis_index("group") * own_rows, own_rows, 0)
    total_entries = width * master.shape[1] * lax.axis_size("mp")
    rms = jnp.sqrt(square_sum / total_entries + 1e-12)
    new_master = master - 0.25 * grad / rms
    renewed16 = new_master.astype(jnp.bfloat16)
    refreshed = add_rows(lax.all_gather(renewed16, "group", axis=0, tiled=True)) * scale
    return (new_master, refreshed.astype(jnp.bfloat16))


def solution(mesh):
    return jax.shard_map(
        shards,
        mesh=mesh,
        in_specs=(P("group", "mp"), P("group", "mp"), P("group", None), P("group", "mp")),
        out_specs=(P("group", "mp"), P("group", "mp")),
        check_vma=False,
    )
```

profile of v0, /device:TPU:1, one launch (start us, length us, event | category | flops | bytes accessed | tf_op | source)
XLA Modules:
  0.0 750.0 jit_solution(8003491488990430044)
XLA Ops:
  7.2 0.0 all-gather.4.cloned.1.call-start
  7.2 0.7 all-gather.4.cloned.1.call-update
  7.9 0.0 all-gather.6.cloned.1.call-start
  7.9 1.6 convert_element_type.38
  9.6 0.0 all-reduce.2.cloned.1.call-start
  9.6 0.7 fusion.13
  10.4 0.1 reshape.22
  10.5 89.2 %all-gather.4.cloned.1.call-done = bf16[256,8192]{1,0:T(8,128)(2,1)} async-done(((bf16[256,512]{1,0:T(8,128)(2,1)}), bf16[256,8192]{1,0:T(8,128)(2,1)}) %all-gather.4.cloned.1.call-update) | async-done | bytes 4194320 | tf_op jit(solution)/shard_map/all_gather | solution.py:10
  99.6 107.7 %all-gather.6.cloned.1.call-done = bf16[8192,256]{1,0:T(8,128)(2,1)} async-done(((bf16[256,256]{1,0:T(8,128)(2,1)}), bf16[8192,256]{1,0:T(8,128)(2,1)}) %all-gather.6.cloned.1.call-update) | async-done | bytes 4194320 | tf_op jit(solution)/shard_map/all_gather | solution.py:18
  207.4 11.3 %fusion.1 = bf16[8192,256]{0,1:T(8,128)(2,1)} fusion(bf16[256,8192]{1,0:T(8,128)(2,1)} %all-gather.4.cloned.1.call-done, bf16[8192,256]{1,0:T(8,128)(2,1)} %all-gather.6.cloned.1.call-done, bf16[256,256]{1,0:T(8,128)(2,1)} %param.5, f32[256]{0:T(256)S(1)} %reshape.22), kind=kOutput, calls=%fused_computation.2 | convolution fusion | flops 2152071168 | bytes 12715008 | tf_op jit(solution)/shard_map/dot_general | solution.py:24
  218.7 0.0 all-reduce.2.cloned.1.call-update
  218.7 0.0 all-gather.8.cloned.1.call-start
  218.8 0.9 copy-done
  219.7 0.1 copy.6
  219.8 370.6 %all-reduce.2.cloned.1.call-done = bf16[8192,256]{0,1:T(8,128)(2,1)} async-done(((bf16[8192,256]{0,1:T(8,128)(2,1)}), bf16[8192,256]{0,1:T(8,128)(2,1)}) %all-reduce.2.cloned.1.call-update) | async-done | bytes 4194320 | tf_op jit(solution)/shard_map/psum | solution.py:27
  590.4 4.9 multiply_reduce_fusion
  595.4 38.5 %psum.15 = f32[]{:T(128)} all-reduce(f32[]{:T(128)} %multiply_reduce_fusion), channel_id=1, replica_groups=mesh['group'=32,'mp'=16] {'mp'}, use_global_device_ids=true, to_apply=%region_2.3 | all-reduce | flops 1 | bytes 8 | tf_op jit(solution)/shard_map/psum | solution.py:28
  634.5 3.2 convert_element_type.45
  637.7 0.7 fusion.17
  638.4 0.0 all-gather.8.cloned.1.call-update
  638.5 0.8 copy.7
  639.3 98.7 %all-gather.8.cloned.1.call-done = bf16[8192,256]{0,1:T(8,128)(2,1)} async-done(((bf16[256,256]{0,1:T(8,128)(2,1)}), bf16[8192,256]{0,1:T(8,128)(2,1)}) %all-gather.8.cloned.1.call-update) | async-done | bytes 4194320 | tf_op jit(solution)/shard_map/all_gather | solution.py:34
  738.0 4.7 fusion.7
  742.7 0.8 copy.8
  (2 shorter events, 0.0 us)
Async XLA Ops:
  7.2 92.5 %all-gather.4.cloned.1.call-start = ((), (), s32[]{:S(2)}) async-start(), calls=%async_computation | async-start | bytes 4456448 | tf_op jit(solution)/shard_map/all_gather | solution.py:10
  7.9 199.5 %all-gather.6.cloned.1.call-start = ((), (), s32[]{:S(2)}) async-start(), calls=%async_computation.1 | async-start | bytes 4325376 | tf_op jit(solution)/shard_map/all_gather | solution.py:18
  9.6 580.8 %all-reduce.2.cloned.1.call-start = ((), (), s32[]{:S(2)}) async-start(), calls=%async_computation.2 | async-start | bytes 8388608 | tf_op jit(solution)/shard_map/psum | solution.py:27
  218.7 0.9 copy-start
  218.7 519.3 %all-gather.8.cloned.1.call-start = ((), (), s32[]{:S(2)}) async-start(), calls=%async_computation.3 | async-start | bytes 4325376 | tf_op jit(solution)/shard_map/all_gather | solution.py:34
Sparse Core Ops, SparseCore 0:
  10.1 89.4 all-gather.3
  103.3 103.9 all-gather.5
  218.8 371.5 all-reduce.1
  638.6 99.3 all-gather.7
where the time goes:
time: 750 us
  waiting for transfers between devices  667 us (89%)
  blocking collectives  38.5 us (5%)
  matrix products  16.1 us (2%)
  between operations  14.5 us (2%)
  other arithmetic  11.2 us (1%)
    psum x1, waiting for transfers between devices, shards(): lax.psum(full_part.astype(jnp.bfloat16), 'group').astype(jnp.float32)  371 us
    all_gather x1, waiting for transfers between devices, shards(): lax.all_gather(weights16, 'group', axis=0, tiled=True)  108 us
    all_gather x1, waiting for transfers between devices, shards(): lax.all_gather(renewed16, 'group', axis=0, tiled=True)  98.7 us
    all_gather x1, waiting for transfers between devices, shards(): x_full = lax.all_gather(hidden, 'mp', axis=1, tiled=True)  89.2 us
    psum x1, blocking collectives, shards(): square_sum = lax.psum(jnp.sum(summed * summed), 'mp')  38.5 us
  transfers between devices with their start and end apart: 4, of which 4 were waited for; matrix products, arithmetic and copies ran while one was open for 0% of the time, Pallas kernels for 0%

commit v1 on v0

v1 whole, which is shorter than its diff:
```python
import jax
import jax.numpy as jnp
from jax import lax
from jax.experimental import pallas as pl
from jax.experimental.pallas import tpu as pltpu
from jax.sharding import PartitionSpec as P

BF = jnp.bfloat16
F32 = jnp.float32
CAP = 256
SLOT = 64
LIVE = 160
REST = CAP - LIVE
B = 256
HB = B // 2
N_COPIES = 160


def shifted(at, **by):
    size = {"y": 4, "zh": 4, "c": 2, "zl": 4, "x": 4}
    return {k: lax.rem(v + by[k] + size[k], size[k]) if k in by else v for k, v in at.items()}


def device(at):
    return ((at["y"] * 4 + at["zh"]) * 2 + at["c"], at["zl"] * 4 + at["x"])


class Copies:
    def __init__(self, send_sem, recv_sem):
        self.send_sem, self.recv_sem, self.used, self.open = send_sem, recv_sem, 0, []

    def new(self, src, dst, to):
        at = self.used
        self.used += 1
        copy = pltpu.make_async_remote_copy(
            src_ref=src,
            dst_ref=dst,
            send_sem=self.send_sem.at[at],
            recv_sem=self.recv_sem.at[at],
            device_id=device(to),
            device_id_type=pl.DeviceIdType.MESH,
        )
        copy.start()
        self.open.append(copy)
        return copy

    def finish(self):
        for copy in self.open:
            copy.wait_send()


class Gather:
    def __init__(self, copies, at, axis, block, halves):
        self.copies, self.axis, self.block, self.halves = copies, axis, block, halves
        self.me = at[axis]
        self.right, self.left = shifted(at, **{axis: 1}), shifted(at, **{axis: -1})

    def start(self):
        mine = self.block(self.me)
        self.to_right = self.copies.new(mine, mine, self.right)
        self.to_left = self.copies.new(mine, mine, self.left)

    def hand_on(self):
        self.to_right.wait_recv()
        half = self.halves(self.block(lax.rem(self.me + 3, 4)))[0]
        self.on_right = self.copies.new(half, half, self.right)
        self.to_left.wait_recv()
        half = self.halves(self.block(lax.rem(self.me + 1, 4)))[1]
        self.on_left = self.copies.new(half, half, self.left)

    def end(self):
        self.on_right.wait_recv()
        self.on_left.wait_recv()


def row_halves(ref):
    return ref.at[pl.ds(0, HB)], ref.at[pl.ds(HB, HB)]


def core_halves(ref):
    return ref.at[0], ref.at[1]


def dot(a, b, contract=((1,), (0,))):
    return lax.dot_general(a, b, (contract, ((), ())), preferred_element_type=F32)


def place_of(row, counts):
    place = jnp.zeros_like(row)
    before = jnp.int32(0)
    for s in range(CAP // SLOT):
        count, inside = counts[s], row - s * SLOT
        valid = inside < count
        to = jnp.where(valid, before + inside, LIVE + s * SLOT - before + inside - count)
        place = jnp.where((row >= s * SLOT) & (row < (s + 1) * SLOT), to, place)
        before = before + count
    return place


def kernel(
    counts_ref, hidden_ref, targets_ref, master_ref, new_ref, out_ref,
    live, rest, cross_live, cross_rest, goal, goal_own, weights, half_pred, other_pred, err,
    part, y_first, y_sum, y_in, z_part, z_first, z_sum, z_in, grad, grad16,
    acc, rest_pred, to_other, from_other, square, squares,
    send_sem, recv_sem,
):
    group, mp = lax.axis_index("group"), lax.axis_index("mp")
    at = {
        "y": group // 8,
        "zh": lax.rem(group // 2, 4),
        "c": lax.rem(group, 2),
        "zl": mp // 4,
        "x": lax.rem(mp, 4),
    }
    y, zh, c, zl, x = at["y"], at["zh"], at["c"], at["zl"], at["x"]
    sibling = shifted(at, c=1)
    copies = Copies(send_sem, recv_sem)
    scale = (32 * B) ** (-0.5)

    barrier = pltpu.get_barrier_semaphore()
    near = [{"c": dc, "x": dx} for dc in range(2) for dx in range(4)][1:]
    stages = [near] + [[{axis: d} for d in (1, 2, 3)] for axis in ("y", "zl", "zh")]
    peers = [by for stage in stages for by in stage]
    for by in peers:
        pl.semaphore_signal(barrier, inc=1, device_id=device(shifted(at, **by)), device_id_type=pl.DeviceIdType.MESH)

    counts = [counts_ref[0, s] for s in range(CAP // SLOT)]
    source = lax.broadcasted_iota(jnp.int32, (CAP, CAP), 1)
    target = lax.broadcasted_iota(jnp.int32, (CAP, CAP), 0)
    to_front = jnp.where(place_of(source, counts) == target, 1.0, 0.0).astype(BF)
    low = dot(to_front, hidden_ref[:, :B]).astype(BF)
    high = dot(to_front, hidden_ref[:, B:]).astype(BF)
    mine, other = jnp.where(c == 0, low, high), jnp.where(c == 0, high, low)
    live[zl, x, c] = mine[:LIVE]
    rest[zl, x, c] = mine[LIVE:]
    cross_live[...] = other[:LIVE]
    cross_rest[...] = other[LIVE:]
    goal_own[...] = dot(to_front, targets_ref[...]).astype(BF)[:LIVE]
    weights[y, zh] = master_ref[...].astype(BF)
    pl.semaphore_wait(barrier, len(peers))

    swap_live = copies.new(cross_live, live.at[zl, x, c], sibling)
    swap_goal = copies.new(goal_own, goal.at[c], sibling)
    swap_rest = copies.new(cross_rest, rest.at[zl, x, c], sibling)

    def gather_rows(buffer):
        over_z = Gather(copies, at, "zh", lambda i: buffer.at[y, i], row_halves)
        over_y = [
            Gather(copies, at, "y", lambda i, k=k: buffer.at[i, lax.rem(zh + k, 4)], row_halves)
            for k in range(4)
        ]
        return over_z, over_y

    def gather_features(buffer):
        over_x = [
            Gather(copies, at, "x", lambda i, k=k: buffer.at[lax.rem(zl + k, 4), i], core_halves)
            for k in range(4)
        ]

        def line():
            mine = buffer.at[zl, x]
            return [copies.new(mine, mine, shifted(at, zl=d)) for d in (3, 2, 1)]

        return line, over_x

    wz, wy = gather_rows(weights)
    wz.start()
    wy[0].start()
    swap_live.wait_recv()
    line, hx = gather_features(live)
    hz = line()
    hx[0].start()
    wy[0].hand_on()
    hx[0].hand_on()
    hz[0].wait_recv()
    hx[1].start()
    hz[2].wait_recv()
    hx[3].start()
    wz.hand_on()
    wy[1].start()
    wy[3].start()
    hz[1].wait_recv()
    hx[2].start()
    hx[1].hand_on()
    hx[3].hand_on()
    wz.end()
    wy[2].start()
    wy[1].hand_on()
    wy[3].hand_on()
    hx[2].hand_on()
    wy[2].hand_on()
    for k in (0, 1, 3, 2):
        hx[k].end()
        wy[k].end()

    half_pred[...] = jnp.zeros_like(half_pred)

    @pl.loop(0, 16)
    def _(b):
        half_pred[...] += dot(live[b // 4, lax.rem(b, 4)].reshape(2 * LIVE, B), weights[b // 4, lax.rem(b, 4)])

    swap_pred = copies.new(half_pred, other_pred, sibling)
    swap_goal.wait_recv()
    goal[c] = goal_own[...]
    swap_pred.wait_recv()
    half_pred_total = half_pred[...] + other_pred[...]
    other_pred[...] = half_pred_total
    diff = jnp.clip(half_pred_total * scale - goal[...].reshape(2 * LIVE, B).astype(F32), -1.0, 1.0)
    err[...] = diff.astype(BF)

    swap_rest.wait_recv()
    rest_line, rx = gather_features(rest)

    def add(*terms):
        total = terms[0].astype(F32)
        for term in terms[1:]:
            total = total + term.astype(F32)
        return total

    def make_parts(k):
        zt = lax.rem(zh + k, 4)

        @pl.loop(0, 4)
        def _(yt):
            h = live[yt, zt].reshape(2 * LIVE, B)
            part[yt, zt] = (dot(h, err[...], ((0,), (0,))) * scale).astype(BF)

    up, down = shifted(at, y=1), shifted(at, y=-1)
    after, before = shifted(at, zh=1), shifted(at, zh=-1)
    yp, ym, yo = lax.rem(y + 1, 4), lax.rem(y + 3, 4), lax.rem(y + 2, 4)
    first, direct, second = {}, {}, {}

    def y_begin(k):
        zt = lax.rem(zh + k, 4)
        h0, h1 = row_halves(part.at[yo, zt])
        first[k] = (copies.new(h0, y_first.at[k, 0], up), copies.new(h1, y_first.at[k, 1], down))
        direct[k] = (
            copies.new(row_halves(part.at[yp, zt])[1], y_in.at[k, 0, 1], up),
            copies.new(row_halves(part.at[ym, zt])[0], y_in.at[k, 1, 0], down),
        )

    def y_middle(k):
        zt = lax.rem(zh + k, 4)
        first[k][0].wait_recv()
        y_sum[k, 0] = add(part[yp, zt, :HB], y_first[k, 0]).astype(BF)
        one = copies.new(y_sum.at[k, 0], y_in.at[k, 0, 0], up)
        first[k][1].wait_recv()
        y_sum[k, 1] = add(part[ym, zt, HB:], y_first[k, 1]).astype(BF)
        second[k] = (one, copies.new(y_sum.at[k, 1], y_in.at[k, 1, 1], down))

    def y_end(k):
        zt = lax.rem(zh + k, 4)
        for copy in direct[k] + second[k]:
            copy.wait_recv()
        total = add(part[y, zt], y_in[k, 0].reshape(B, B), y_in[k, 1].reshape(B, B))
        if k == 0:
            grad[...] = total
        else:
            z_part[k] = total.astype(BF)

    make_parts(2)
    y_begin(2)
    make_parts(1)
    y_begin(1)
    make_parts(3)
    y_begin(3)
    make_parts(0)
    y_middle(2)
    y_begin(0)
    y_end(2)
    h0, h1 = row_halves(z_part.at[2])
    z_first_copies = (copies.new(h0, z_first.at[0], after), copies.new(h1, z_first.at[1], before))
    rz = rest_line()
    rx[0].start()
    y_middle(1)
    y_middle(3)
    y_end(1)
    z_direct = [copies.new(row_halves(z_part.at[1])[1], z_in.at[0, 1], after)]
    y_end(3)
    z_direct.append(copies.new(row_halves(z_part.at[3])[0], z_in.at[1, 0], before))
    y_middle(0)
    z_first_copies[0].wait_recv()
    z_sum[0] = add(z_part[1, :HB], z_first[0]).astype(BF)
    z_direct.append(copies.new(z_sum.at[0], z_in.at[0, 0], after))
    z_first_copies[1].wait_recv()
    z_sum[1] = add(z_part[3, HB:], z_first[1]).astype(BF)
    z_direct.append(copies.new(z_sum.at[1], z_in.at[1, 1], before))
    y_end(0)
    rx[0].hand_on()
    rz[0].wait_recv()
    rx[1].start()
    rz[2].wait_recv()
    rx[3].start()
    rz[1].wait_recv()
    rx[2].start()
    rx[1].hand_on()
    rx[3].hand_on()
    for copy in z_direct:
        copy.wait_recv()
    grad[...] = add(grad[...], z_in[0].reshape(B, B), z_in[1].reshape(B, B))
    grad16[y, zh] = grad[...].astype(BF)

    gz, gy = gather_rows(grad16)
    gz.start()
    gy[0].start()

    total = jnp.sum(grad[...] * grad[...])
    square_copies = []

    def square_begin(s, total):
        square[s] = jnp.full((8, 128), total, F32)
        square_copies.append(
            [copies.new(square.at[s], squares.at[s, j], shifted(at, **by)) for j, by in enumerate(stages[s])]
        )

    def square_end(s):
        total = square[s]
        for j, copy in enumerate(square_copies[s]):
            copy.wait_recv()
            total = total + squares[s, j]
        return total[0, 0]

    square_begin(0, total)
    rx[2].hand_on()
    total = square_end(0)
    square_begin(1, total)
    gy[0].hand_on()
    total = square_end(1)
    square_begin(2, total)
    for k in range(4):
        rx[k].end()
    rest_pred[...] = jnp.zeros_like(rest_pred)
    acc[...] = jnp.zeros_like(acc)

    @pl.loop(0, 16)
    def _(b):
        rest_pred[...] += dot(rest[b // 4, lax.rem(b, 4)].reshape(2 * REST, B), weights[b // 4, lax.rem(b, 4)])

    def use(k):
        zt = lax.rem(zh + k, 4)

        @pl.loop(0, 4)
        def _(yt):
            g = grad16[yt, zt]
            acc[: 2 * LIVE] += dot(live[yt, zt].reshape(2 * LIVE, B), g)
            acc[2 * LIVE :] += dot(rest[yt, zt].reshape(2 * REST, B), g)

    total = square_end(2)
    square_begin(3, total)
    gz.hand_on()
    gy[1].start()
    gy[3].start()
    gy[0].end()
    use(0)
    gz.end()
    gy[2].start()
    gy[1].hand_on()
    gy[3].hand_on()
    total = square_end(3)
    rms = jnp.sqrt(jnp.full((8, 128), total, F32) / (32 * B * 16 * B) + 1e-12)
    step = (0.25 / rms)[0, 0]
    new_ref[...] = master_ref[...] - step * grad[...]
    gy[2].hand_on()
    for k in (1, 3, 2):
        gy[k].end()
        use(k)

    o = 1 - c
    live_at, rest_at = pl.multiple_of(c * LIVE, 8), pl.multiple_of(2 * LIVE + c * REST, 8)
    live_of, rest_of = pl.multiple_of(o * LIVE, 8), pl.multiple_of(2 * LIVE + o * REST, 8)
    to_other[:LIVE] = step * acc[pl.ds(live_of, LIVE)]
    to_other[LIVE:] = step * acc[pl.ds(rest_of, REST)] - rest_pred[pl.ds(pl.multiple_of(o * REST, 8), REST)]
    swap_out = copies.new(to_other, from_other, sibling)
    own_live = other_pred[pl.ds(live_at, LIVE)] - step * acc[pl.ds(live_at, LIVE)]
    own_rest = rest_pred[pl.ds(pl.multiple_of(c * REST, 8), REST)] - step * acc[pl.ds(rest_at, REST)]
    swap_out.wait_recv()
    own = jnp.concatenate([own_live - from_other[:LIVE], own_rest - from_other[LIVE:]], axis=0)
    out_ref[...] = dot(to_front, (own * scale).astype(BF), ((0,), (0,))).astype(BF)
    copies.finish()


def shards(hidden, targets, counts, master):
    vmem, bf, f32 = pltpu.VMEM, BF, F32
    return pl.pallas_call(
        kernel,
        out_shape=(jax.ShapeDtypeStruct((B, B), F32), jax.ShapeDtypeStruct((CAP, B), BF)),
        in_specs=[pl.BlockSpec(memory_space=pltpu.SMEM)] + [pl.BlockSpec(memory_space=vmem)] * 3,
        out_specs=[pl.BlockSpec(memory_space=vmem)] * 2,
        scratch_shapes=[
            vmem((4, 4, 2, LIVE, B), bf),
            vmem((4, 4, 2, REST, B), bf),
            vmem((LIVE, B), bf),
            vmem((REST, B), bf),
            vmem((2, LIVE, B), bf),
            vmem((LIVE, B), bf),
            vmem((4, 4, B, B), bf),
            vmem((2 * LIVE, B), f32),
            vmem((2 * LIVE, B), f32),
            vmem((2 * LIVE, B), bf),
            vmem((4, 4, B, B), bf),
            vmem((4, 2, HB, B), bf),
            vmem((4, 2, HB, B), bf),
            vmem((4, 2, 2, HB, B), bf),
            vmem((4, B, B), bf),
            vmem((2, HB, B), bf),
            vmem((2, HB, B), bf),
            vmem((2, 2, HB, B), bf),
            vmem((B, B), f32),
            vmem((4, 4, B, B), bf),
            vmem((2 * CAP, B), f32),
            vmem((2 * REST, B), f32),
            vmem((CAP, B), f32),
            vmem((CAP, B), f32),
            vmem((4, 8, 128), f32),
            vmem((4, 7, 8, 128), f32),
            pltpu.SemaphoreType.DMA((N_COPIES,)),
            pltpu.SemaphoreType.DMA((N_COPIES,)),
        ],
        compiler_params=pltpu.CompilerParams(
            collective_id=0, has_side_effects=True, vmem_limit_bytes=40 * 1024 * 1024
        ),
        name="recalibrate",
    )(counts, hidden, targets, master)


def solution(mesh):
    return jax.shard_map(
        shards,
        mesh=mesh,
        in_specs=(P("group", "mp"), P("group", "mp"), P("group", None), P("group", "mp")),
        out_specs=(P("group", "mp"), P("group", "mp")),
        check_vma=False,
    )
```

time: 750 us -> 150 us (0.20)
  waiting for transfers between devices: 667 us -> 0 us
  Pallas kernels: 0 us -> 142 us
  blocking collectives: 38.5 us -> 0 us
  matrix products: 16.1 us -> 0 us
  between operations: 14.5 us -> 0.65 us
  other arithmetic: 11.2 us -> 0 us
    psum x1 -> x0, waiting for transfers between devices: 371 us -> none  [shards(): lax.psum(full_part.astype(jnp.bfloat16), 'group').astype(jnp.float32)]
    all_gather x3 -> x0, waiting for transfers between devices: 296 us -> none  [the longest x1 108 us: shards(): lax.all_gather(weights16, 'group', axis=0, tiled=True)]
    pallas_call x0 -> x1, Pallas kernels: none -> 142 us  [shards(): pl.pallas_call(kernel, out_shape=(jax.ShapeDtypeStruct((B, B), F32), jax....]
    psum x1 -> x0, blocking collectives: 38.5 us -> none  [shards(): square_sum = lax.psum(jnp.sum(summed * summed), 'mp')]
    dot_general x2 -> x0, matrix products: 16.1 us -> none  [the longest x1 11.3 us: shards(): lax.dot_general(x_full, err, (((0,), (0,)), ((), ())), preferred_element_...]
  transfers between devices with their start and end apart: 4 -> 0, of which waited for: 4 -> 0; matrix products, arithmetic and copies ran while one was open for 0% -> 0% of each run, Pallas kernels for 0% -> 0%
where the time goes in v1:
time: 150 us; the launch traced here: 147 us
  Pallas kernels  142 us (95%)
  local copies, waits for them, and re-layouts  4.81 us (3%)
    pallas_call x1, Pallas kernels, shards(): pl.pallas_call(kernel, out_shape=(jax.ShapeDtypeStruct((B, B), F32), jax....  142 us
    unnamed x10, local copies, waits for them, and re-layouts  4.81 us

profile of v1, /device:TPU:1, one launch (start us, length us, event | category | flops | bytes accessed | tf_op | source)
XLA Modules:
  0.0 147.2 jit_solution(17394586580677808207)
XLA Ops:
  0.6 0.0 copy-start
  0.6 0.9 copy-done
  1.6 0.0 copy-start.1
  1.6 0.9 copy-done.1
  2.5 0.0 copy-start.2
  2.5 0.9 copy-done.2
  3.4 0.0 copy-start.3
  3.4 0.7 copy-done.3
  4.1 141.7 %recalibrate.1 = (f32[256,256]{1,0:T(8,128)S(1)}, bf16[256,256]{1,0:T(8,128)(2,1)S(1)}) custom-call(s32[1,4]{1,0:T(1,128)S(1)} %copy-done.3, bf16[256,512]{1,0:T(8,128)(2,1)S(1)} %copy-done, bf16[256,256]{1,0:T(8,128)(2,1)S(1)} %copy-done.2, f32[256,256]{1,0:T(8,128)S(1)} %copy-done.1), custom_call_target="tpu_custom_call" | custom-call | tf_op jit(solution)/shard_map/recalibrate/pallas_call | solution.py:384
  145.8 0.7 copy.8
  146.5 0.7 copy.9
Async XLA Ops:
  0.6 1.0 copy-start
  1.6 0.9 copy-start.1
  2.5 0.9 copy-start.2
  3.4 0.7 copy-start.3

commit v2 on v0

v2 whole, which is shorter than its diff:
```python
import jax
import jax.numpy as jnp
from jax import lax
from jax.experimental import pallas as pl
from jax.experimental.pallas import tpu as pltpu
from jax.sharding import PartitionSpec as P

BF = jnp.bfloat16
F32 = jnp.float32
CAP = 256
SLOT = 64
LIVE = 160
REST = CAP - LIVE
B = 256
HB = B // 2
N = B // 2
N_COPIES = 256
MESH = pl.DeviceIdType.MESH


def shifted(at, **by):
    size = {"y": 4, "zh": 4, "c": 2, "zl": 4, "x": 4}
    return {k: lax.rem(v + by[k] + size[k], size[k]) if k in by else v for k, v in at.items()}


def device(at):
    return ((at["y"] * 4 + at["zh"]) * 2 + at["c"], at["zl"] * 4 + at["x"])


class Copies:
    def __init__(self, send_sem, recv_sem):
        self.send_sem, self.recv_sem, self.used, self.open, self.conditional = send_sem, recv_sem, 0, [], []

    def make(self, src, dst, to, recv_sem=None):
        at = self.used
        self.used += 1
        copy = pltpu.make_async_remote_copy(
            src_ref=src,
            dst_ref=dst,
            send_sem=self.send_sem.at[at],
            recv_sem=self.recv_sem.at[at] if recv_sem is None else recv_sem,
            device_id=device(to),
            device_id_type=MESH,
        )
        return copy

    def new(self, src, dst, to):
        copy = self.make(src, dst, to)
        copy.start()
        self.open.append(copy)
        return copy

    def new_if(self, condition, src, dst, to, recv_sem):
        copy = self.make(src, dst, to, recv_sem)
        pl.when(condition)(lambda: copy.start())
        self.conditional.append((condition, copy))

    def finish(self):
        for copy in self.open:
            copy.wait_send()
        for condition, copy in self.conditional:
            pl.when(condition)(lambda copy=copy: copy.wait_send())


class Gather:
    def __init__(self, copies, at, axis, block, halves, split=False):
        self.copies, self.block, self.halves, self.split = copies, block, halves, split
        self.me = at[axis]
        self.right, self.left = shifted(at, **{axis: 1}), shifted(at, **{axis: -1})
        self.of_left, self.of_right = lax.rem(self.me + 3, 4), lax.rem(self.me + 1, 4)

    def start(self):
        mine = self.block(self.me)
        if self.split:
            h0, h1 = self.halves(mine)
            self.to_right = self.copies.new(h0, h0, self.right)
            self.to_left = self.copies.new(h1, h1, self.left)
        else:
            self.to_right = self.copies.new(mine, mine, self.right)
            self.to_left = self.copies.new(mine, mine, self.left)

    def start_late(self):
        h0, h1 = self.halves(self.block(self.me))
        self.late = [self.copies.new(h1, h1, self.right), self.copies.new(h0, h0, self.left)]

    def hand_on(self):
        self.to_right.wait_recv()
        half = self.halves(self.block(self.of_left))[0]
        self.on_right = self.copies.new(half, half, self.right)
        self.to_left.wait_recv()
        half = self.halves(self.block(self.of_right))[1]
        self.on_left = self.copies.new(half, half, self.left)

    def near(self):
        for copy in self.late:
            copy.wait_recv()

    def end(self):
        self.on_right.wait_recv()
        self.on_left.wait_recv()


class Spread:
    def __init__(self, copies, at, axis, block):
        self.copies, self.mine = copies, block(at[axis])
        self.others = [shifted(at, **{axis: d}) for d in (1, 3, 2)]

    def start(self):
        self.sent = [self.copies.new(self.mine, self.mine, to) for to in self.others]

    def end(self):
        for copy in self.sent:
            copy.wait_recv()


class Line:
    def __init__(self, copies, at, block, sems):
        self.copies, self.at, self.block, self.sems = copies, at, block, sems
        zl = self.zl = at["zl"]
        self.middle = (zl == 1) | (zl == 2)
        low = zl == 1
        self.order = [
            jnp.where(zl == 0, 1, jnp.where(zl == 3, 3, jnp.where(low, 3, 1))),
            jnp.where(zl == 0, 2, jnp.where(zl == 3, 2, jnp.where(low, 1, 3))),
            jnp.where(zl == 0, 3, jnp.where(zl == 3, 1, 2)),
        ]
        self.step = [jnp.where(low, 1, -1), jnp.where(low, -1, 1), jnp.where(low, -1, 1)]
        self.lands = [2, 2, jnp.where(low, 3, 1)]

    def send(self, condition, zl, to, lands):
        ref = self.block(zl)
        self.copies.new_if(condition, ref, ref, {**self.at, "zl": to}, self.sems.at[lands])

    def start(self):
        zl = self.zl
        self.send(zl < 3, zl, lax.min(zl + 1, 3), 3)
        self.send(zl > 0, zl, lax.max(zl - 1, 0), 1)

    def slot(self, s):
        return lax.rem(self.zl + self.order[s], 4)

    def arrive(self, s):
        zl = self.slot(s)
        ref = self.block(zl)
        pltpu.make_async_copy(ref, ref, self.sems.at[self.order[s]]).wait()
        to = jnp.where(self.middle, self.zl + self.step[s], 1)
        self.send(self.middle, zl, to, self.lands[s])


def row_halves(ref):
    return ref.at[pl.ds(0, HB)], ref.at[pl.ds(HB, HB)]


def live_halves(ref):
    return ref.at[pl.ds(0, LIVE // 2)], ref.at[pl.ds(LIVE // 2, LIVE // 2)]


def dot(a, b, contract=((1,), (0,))):
    return lax.dot_general(a, b, (contract, ((), ())), preferred_element_type=F32)


def add(*terms):
    total = terms[0].astype(F32)
    for term in terms[1:]:
        total = total + term.astype(F32)
    return total


def place_of(row, counts):
    place = jnp.zeros_like(row)
    before = jnp.int32(0)
    for s in range(CAP // SLOT):
        count, inside = counts[s], row - s * SLOT
        valid = inside < count
        to = jnp.where(valid, before + inside, LIVE + s * SLOT - before + inside - count)
        place = jnp.where((row >= s * SLOT) & (row < (s + 1) * SLOT), to, place)
        before = before + count
    return place


def kernel(
    counts_ref, hidden_hbm, targets_hbm, master_hbm, new_ref, out_ref,
    hidden_ref, targets_ref, master_ref,
    live, rest, cross_live, cross_rest, goal, goal_own, weights, half_pred, other_pred, err,
    part, y_in, z_part, z_first, z_sum, z_in, grad, grad16,
    acc, rest_pred, to_other, from_other, square, squares,
    send_sem, recv_sem, line_sem, load_sem,
):
    group, mp = lax.axis_index("group"), lax.axis_index("mp")
    at = {
        "y": group // 8,
        "zh": lax.rem(group // 2, 4),
        "c": lax.rem(group, 2),
        "zl": mp // 4,
        "x": lax.rem(mp, 4),
    }
    y, zh, c, zl, x = at["y"], at["zh"], at["c"], at["zl"], at["x"]
    sibling = shifted(at, c=1)
    copies = Copies(send_sem, recv_sem)
    scale = (32 * B) ** (-0.5)

    barrier = pltpu.get_barrier_semaphore()
    near = [{"c": dc, "x": dx} for dc in range(2) for dx in range(4)][1:]
    stages = [near] + [[{axis: d} for d in (1, 2, 3)] for axis in ("y", "zl")]
    peers = [by for stage in stages for by in stage] + [{"zh": 1}, {"zh": -1}]
    for by in reversed(peers):
        pl.semaphore_signal(barrier, inc=1, device_id=device(shifted(at, **by)), device_id_type=MESH)
    loads = [
        pltpu.make_async_copy(src, dst, load_sem.at[i])
        for i, (src, dst) in enumerate(
            [(master_hbm, master_ref), (hidden_hbm, hidden_ref), (targets_hbm, targets_ref)]
        )
    ]
    for load in loads:
        load.start()
    loads[0].wait()
    for h in range(2):
        weights[h, y, zh] = master_ref[:, h * N : (h + 1) * N].astype(BF)

    def gather_rows(buffer, h):
        over_z = Gather(copies, at, "zh", lambda i: buffer.at[h, y, i], row_halves, split=True)
        over_y = [
            Spread(copies, at, "y", lambda i, k=k: buffer.at[h, i, lax.rem(zh + k, 4)]) for k in range(4)
        ]
        return over_z, over_y

    counts = [counts_ref[0, s] for s in range(CAP // SLOT)]
    place = place_of(lax.broadcasted_iota(jnp.int32, (8, CAP), 1), counts)[:1]
    target = lax.broadcasted_iota(jnp.int32, (CAP, CAP), 0)
    to_front = jnp.where(place == target, 1.0, 0.0).astype(BF)
    loads[1].wait()
    low = dot(to_front, hidden_ref[:, :B]).astype(BF)
    high = dot(to_front, hidden_ref[:, B:]).astype(BF)
    mine, other = jnp.where(c == 0, low, high), jnp.where(c == 0, high, low)
    cross_live[...] = other[:LIVE]
    cross_rest[...] = other[LIVE:]
    live[zl, x, c] = mine[:LIVE]
    rest[zl, x, c] = mine[LIVE:]
    (wz, wy), (vz, vy) = [gather_rows(weights, h) for h in range(2)]
    pl.semaphore_wait(barrier, len(peers))
    wz.start()
    wy[0].start()

    swap_live = copies.new(cross_live, live.at[zl, x, c], sibling)

    o = 1 - c
    a = Line(copies, at, lambda i: live.at[i, x, c], line_sem.at[0])
    b = Line(copies, at, lambda i: live.at[i, x, o], line_sem.at[1])
    places = [zl] + [a.slot(s) for s in range(3)]
    ax = [Gather(copies, at, "x", lambda i, p=p: live.at[p, i, c], live_halves) for p in places]
    bx = [Gather(copies, at, "x", lambda i, p=p: live.at[p, i, o], live_halves) for p in places]
    a.start()
    ax[0].start()
    loads[2].wait()
    goal_own[...] = dot(to_front, targets_ref[...]).astype(BF)[:LIVE]
    swap_goal = copies.new(goal_own, goal.at[c], sibling)
    swap_rest = copies.new(cross_rest, rest.at[zl, x, c], sibling)
    goal[c] = goal_own[...]
    swap_live.wait_recv()
    b.start()
    bx[0].start()
    wz.start_late()

    def predict(h):
        total = jnp.zeros((2 * LIVE, N), F32)
        for b in range(16):
            total = total + dot(live[b // 4, b % 4].reshape(2 * LIVE, B), weights[h, b // 4, b % 4])
        half_pred[h] = total
        return copies.new(half_pred.at[h], other_pred.at[h], sibling)

    def errors(h):
        total = half_pred[h] + other_pred[h]
        other_pred[h] = total
        wanted = goal[:, :, h * N : (h + 1) * N].reshape(2 * LIVE, N).astype(F32)
        err[h] = jnp.clip(total * scale - wanted, -1.0, 1.0).astype(BF)

    def predict_rest(h):
        total = jnp.zeros((2 * REST, N), F32)
        for b in range(16):
            total = total + dot(rest[b // 4, b % 4].reshape(2 * REST, B), weights[h, b // 4, b % 4])
        rest_pred[h] = total

    after, before = shifted(at, zh=1), shifted(at, zh=-1)

    class Reduce:
        def __init__(self, h):
            self.h, self.sent, self.z_direct = h, {}, []

        def parts(self, k):
            zt = lax.rem(zh + k, 4)
            e = err[self.h]
            for yt in range(4):
                rows = live[yt, zt].reshape(2 * LIVE, B)
                part[self.h, yt, zt] = (dot(rows, e, ((0,), (0,))) * scale).astype(BF)

        def begin(self, k):
            h, zt = self.h, lax.rem(zh + k, 4)
            self.sent[k] = [
                copies.new(part.at[h, lax.rem(y + d, 4), zt], y_in.at[h, k, d - 1], shifted(at, y=d))
                for d in (1, 3, 2)
            ]

        def end(self, k):
            h, zt = self.h, lax.rem(zh + k, 4)
            for copy in self.sent[k]:
                copy.wait_recv()
            total = add(part[h, y, zt], y_in[h, k, 0], y_in[h, k, 1], y_in[h, k, 2])
            if k == 0:
                grad[h] = total
                return
            z_part[h, k] = total.astype(BF)
            h0, h1 = row_halves(z_part.at[h, k])
            if k == 2:
                self.z_first = (
                    copies.new(h0, z_first.at[h, 0], after),
                    copies.new(h1, z_first.at[h, 1], before),
                )
            elif k == 1:
                self.z_direct.append(copies.new(h1, z_in.at[h, 0, 1], after))
            else:
                self.z_direct.append(copies.new(h0, z_in.at[h, 1, 0], before))

        def z_middle(self):
            h = self.h
            self.z_first[0].wait_recv()
            z_sum[h, 0] = add(z_part[h, 1, :HB], z_first[h, 0]).astype(BF)
            self.z_direct.append(copies.new(z_sum.at[h, 0], z_in.at[h, 0, 0], after))
            self.z_first[1].wait_recv()
            z_sum[h, 1] = add(z_part[h, 3, HB:], z_first[h, 1]).astype(BF)
            self.z_direct.append(copies.new(z_sum.at[h, 1], z_in.at[h, 1, 1], before))

        def z_end(self):
            h = self.h
            for copy in self.z_direct:
                copy.wait_recv()
            grad[h] = add(grad[h], z_in[h, 0].reshape(B, N), z_in[h, 1].reshape(B, N))
            grad16[h, y, zh] = grad[h].astype(BF)

    def use(h, k):
        zt = lax.rem(zh + k, 4)
        top = acc[h, : 2 * LIVE] if k else jnp.zeros((2 * LIVE, N), F32)
        low = acc[h, 2 * LIVE :] if k else jnp.zeros((2 * REST, N), F32)
        for yt in range(4):
            g = grad16[h, yt, zt]
            top = top + dot(live[yt, zt].reshape(2 * LIVE, B), g)
            low = low + dot(rest[yt, zt].reshape(2 * REST, B), g)
        acc[h, : 2 * LIVE] = top
        acc[h, 2 * LIVE :] = low

    a.arrive(0)
    ax[1].start()
    ax[0].hand_on()
    b.arrive(0)
    bx[1].start()
    bx[0].hand_on()
    wz.hand_on()
    vz.start()
    vy[0].start()
    a.arrive(1)
    ax[2].start()
    ax[1].hand_on()
    b.arrive(1)
    bx[2].start()
    bx[1].hand_on()
    wz.near()
    wy[1].start()
    wy[3].start()
    vz.start_late()
    a.arrive(2)
    ax[3].start()
    ax[2].hand_on()
    b.arrive(2)
    bx[3].start()
    bx[2].hand_on()
    wz.end()
    wy[2].start()
    vz.hand_on()
    ax[3].hand_on()
    bx[3].hand_on()
    for k in range(4):
        ax[k].end()
        bx[k].end()
        wy[k].end()

    swap_pred = predict(0)
    vz.near()
    vy[1].start()
    vy[3].start()
    swap_rest.wait_recv()
    swap_goal.wait_recv()
    rest_line = Line(copies, at, lambda i: rest.at[i, x], line_sem.at[2])
    rx = [Spread(copies, at, "x", lambda i, p=p: rest.at[p, i]) for p in places]
    rest_line.start()
    rx[0].start()
    swap_pred.wait_recv()
    errors(0)
    r0, r1 = Reduce(0), Reduce(1)
    r0.parts(2)
    r0.begin(2)
    r0.parts(1)
    r0.parts(3)
    r0.parts(0)
    vz.end()
    vy[2].start()
    r0.begin(1)
    r0.begin(3)
    r0.end(2)
    r0.begin(0)
    for k in range(4):
        vy[k].end()
    swap_pred = predict(1)
    rest_line.arrive(0)
    rx[1].start()
    r0.end(1)
    r0.end(3)
    swap_pred.wait_recv()
    errors(1)
    r1.parts(2)
    r1.begin(2)
    r0.z_middle()
    r1.parts(1)
    r1.parts(3)
    r1.parts(0)
    r1.begin(1)
    r1.begin(3)
    r0.end(0)
    r1.end(2)
    r1.begin(0)
    rest_line.arrive(1)
    rx[2].start()
    r0.z_end()
    (gz, gy), (fz, fy) = [gather_rows(grad16, h) for h in range(2)]
    gz.start()
    gz.start_late()
    gy[0].start()
    r1.end(1)
    r1.end(3)
    rest_line.arrive(2)
    rx[3].start()
    r1.z_middle()
    r1.end(0)
    gz.hand_on()
    gz.near()
    gy[1].start()
    gy[3].start()
    for k in range(4):
        rx[k].end()
    predict_rest(0)
    predict_rest(1)
    r1.z_end()
    fz.start()
    fz.start_late()
    fy[0].start()

    def square_begin(s, total):
        square[s] = jnp.full((8, 128), total, F32)
        return [copies.new(square.at[s], squares.at[s, j], shifted(at, **by)) for j, by in enumerate(stages[s])]

    def square_end(s, sent):
        total = square[s]
        for j, copy in enumerate(sent):
            copy.wait_recv()
            total = total + squares[s, j]
        return total[0, 0]

    total = jnp.sum(grad[0] * grad[0] + grad[1] * grad[1])
    sent = square_begin(0, total)
    gy[0].end()
    use(0, 0)
    gz.end()
    gy[2].start()
    sent = square_begin(1, square_end(0, sent))
    gy[1].end()
    use(0, 1)
    sent = square_begin(2, square_end(1, sent))
    gy[3].end()
    use(0, 3)
    fz.hand_on()
    total = square_end(2, sent)
    square[3] = jnp.full((8, 128), total, F32)
    ring = [copies.new(square.at[3], squares.at[3, 0], after), copies.new(square.at[3], squares.at[3, 1], before)]
    fz.near()
    fy[1].start()
    fy[3].start()
    gy[2].end()
    use(0, 2)
    fy[0].end()
    use(1, 0)
    ring[0].wait_recv()
    ring.append(copies.new(squares.at[3, 0], squares.at[3, 2], after))
    fz.end()
    fy[2].start()
    fy[1].end()
    use(1, 1)
    fy[3].end()
    use(1, 3)
    ring[1].wait_recv()
    ring[2].wait_recv()
    total = (square[3] + squares[3, 0]) + (squares[3, 1] + squares[3, 2])
    rms = jnp.sqrt(total / (32 * B * 16 * B) + 1e-12)
    step = (0.25 / rms)[0, 0]
    for h in range(2):
        new_ref[:, h * N : (h + 1) * N] = master_ref[:, h * N : (h + 1) * N] - step * grad[h]

    live_at, rest_at = pl.multiple_of(c * LIVE, 8), pl.multiple_of(c * REST, 8)
    live_of, rest_of = pl.multiple_of(o * LIVE, 8), pl.multiple_of(o * REST, 8)
    more = 2 * LIVE

    def give(h):
        to_other[h, :LIVE] = step * acc[h, pl.ds(live_of, LIVE)]
        to_other[h, LIVE:] = step * acc[h, pl.ds(more + rest_of, REST)] - rest_pred[h, pl.ds(rest_of, REST)]
        return copies.new(to_other.at[h], from_other.at[h], sibling)

    def take(h, swap):
        own_live = other_pred[h, pl.ds(live_at, LIVE)] - step * acc[h, pl.ds(live_at, LIVE)]
        own_rest = rest_pred[h, pl.ds(rest_at, REST)] - step * acc[h, pl.ds(more + rest_at, REST)]
        swap.wait_recv()
        own = jnp.concatenate([own_live - from_other[h, :LIVE], own_rest - from_other[h, LIVE:]], axis=0)
        out_ref[:, h * N : (h + 1) * N] = dot(to_front, (own * scale).astype(BF), ((0,), (0,))).astype(BF)

    take(0, give(0))
    fy[2].end()
    use(1, 2)
    take(1, give(1))
    copies.finish()


def shards(hidden, targets, counts, master):
    vmem, bf, f32 = pltpu.VMEM, BF, F32
    return pl.pallas_call(
        kernel,
        out_shape=(jax.ShapeDtypeStruct((B, B), F32), jax.ShapeDtypeStruct((CAP, B), BF)),
        in_specs=[pl.BlockSpec(memory_space=pltpu.SMEM)] + [pl.BlockSpec(memory_space=pl.ANY)] * 3,
        out_specs=[pl.BlockSpec(memory_space=vmem)] * 2,
        scratch_shapes=[
            vmem((CAP, 2 * B), bf),
            vmem((CAP, B), bf),
            vmem((B, B), f32),
            vmem((4, 4, 2, LIVE, B), bf),
            vmem((4, 4, 2, REST, B), bf),
            vmem((LIVE, B), bf),
            vmem((REST, B), bf),
            vmem((2, LIVE, B), bf),
            vmem((LIVE, B), bf),
            vmem((2, 4, 4, B, N), bf),
            vmem((2, 2 * LIVE, N), f32),
            vmem((2, 2 * LIVE, N), f32),
            vmem((2, 2 * LIVE, N), bf),
            vmem((2, 4, 4, B, N), bf),
            vmem((2, 4, 3, B, N), bf),
            vmem((2, 4, B, N), bf),
            vmem((2, 2, HB, N), bf),
            vmem((2, 2, HB, N), bf),
            vmem((2, 2, 2, HB, N), bf),
            vmem((2, B, N), f32),
            vmem((2, 4, 4, B, N), bf),
            vmem((2, 2 * CAP, N), f32),
            vmem((2, 2 * REST, N), f32),
            vmem((2, CAP, N), f32),
            vmem((2, CAP, N), f32),
            vmem((4, 8, 128), f32),
            vmem((4, 7, 8, 128), f32),
            pltpu.SemaphoreType.DMA((N_COPIES,)),
            pltpu.SemaphoreType.DMA((N_COPIES,)),
            pltpu.SemaphoreType.DMA((3, 4)),
            pltpu.SemaphoreType.DMA((3,)),
        ],
        compiler_params=pltpu.CompilerParams(
            collective_id=0, has_side_effects=True, vmem_limit_bytes=56 * 1024 * 1024
        ),
        name="recalibrate",
    )(counts, hidden, targets, master)


def solution(mesh):
    return jax.shard_map(
        shards,
        mesh=mesh,
        in_specs=(P("group", "mp"), P("group", "mp"), P("group", None), P("group", "mp")),
        out_specs=(P("group", "mp"), P("group", "mp")),
        check_vma=False,
    )
```

time: 750 us -> 131 us (0.17)
  waiting for transfers between devices: 667 us -> 0 us
  Pallas kernels: 0 us -> 128 us
  blocking collectives: 38.5 us -> 0 us
  matrix products: 16.1 us -> 0 us
  between operations: 14.5 us -> 0.65 us
  other arithmetic: 11.2 us -> 0 us
    psum x1 -> x0, waiting for transfers between devices: 371 us -> none  [shards(): lax.psum(full_part.astype(jnp.bfloat16), 'group').astype(jnp.float32)]
    all_gather x3 -> x0, waiting for transfers between devices: 296 us -> none  [the longest x1 108 us: shards(): lax.all_gather(weights16, 'group', axis=0, tiled=True)]
    pallas_call x0 -> x1, Pallas kernels: none -> 128 us  [shards(): pl.pallas_call(kernel, out_shape=(jax.ShapeDtypeStruct((B, B), F32), jax....]
    psum x1 -> x0, blocking collectives: 38.5 us -> none  [shards(): square_sum = lax.psum(jnp.sum(summed * summed), 'mp')]
    dot_general x2 -> x0, matrix products: 16.1 us -> none  [the longest x1 11.3 us: shards(): lax.dot_general(x_full, err, (((0,), (0,)), ((), ())), preferred_element_...]
  transfers between devices with their start and end apart: 4 -> 0, of which waited for: 4 -> 0; matrix products, arithmetic and copies ran while one was open for 0% -> 0% of each run, Pallas kernels for 0% -> 0%
where the time goes in v2:
time: 131 us
  Pallas kernels  128 us (98%)
  local copies, waits for them, and re-layouts  2.36 us (2%)
    pallas_call x1, Pallas kernels, shards(): pl.pallas_call(kernel, out_shape=(jax.ShapeDtypeStruct((B, B), F32), jax....  128 us

profile of v2, /device:TPU:1, one launch (start us, length us, event | category | flops | bytes accessed | tf_op | source)
XLA Modules:
  0.0 131.2 jit_solution(16468549703909697172)
XLA Ops:
  0.6 128.2 %recalibrate.1 = (f32[256,256]{1,0:T(8,128)}, bf16[256,256]{1,0:T(8,128)(2,1)}) custom-call(s32[1,4]{1,0:T(1,128)} %counts_ref.1, bf16[256,512]{1,0:T(8,128)(2,1)} %hidden_hbm.1, bf16[256,256]{1,0:T(8,128)(2,1)} %targets_hbm.1, f32[256,256]{1,0:T(8,128)} %master_hbm.1), custom_call_target="tpu_custom_call" | custom-call | tf_op jit(solution)/shard_map/recalibrate/pallas_call | solution.py:530
  128.8 0.0 copy-start
  128.8 1.7 %copy.8 = f32[256,256]{1,0:T(8,128)} copy(f32[256,256]{1,0:T(8,128)} %get-tuple-element.4) | data formatting | bytes 524288
  130.5 0.0 copy-done
  130.5 0.7 copy.9
Async XLA Ops:
  128.8 1.7 %copy-start = (bf16[256,256]{1,0:T(8,128)(2,1)S(1)}, bf16[256,256]{1,0:T(8,128)(2,1)}, u32[]{:S(2)}) copy-start(bf16[256,256]{1,0:T(8,128)(2,1)} %get-tuple-element.5) | copy-start | bytes 393220

commit v3 on v2

--- a/solution.py
+++ b/solution.py
@@ -377,17 +377,19 @@
     vz.hand_on()
     ax[3].hand_on()
     bx[3].hand_on()
+    vz.near()
+    vy[1].start()
+    vy[3].start()
     for k in range(4):
         ax[k].end()
         bx[k].end()
         wy[k].end()
 
     swap_pred = predict(0)
-    vz.near()
-    vy[1].start()
-    vy[3].start()
     swap_rest.wait_recv()
     swap_goal.wait_recv()
+    vz.end()
+    vy[2].start()
     rest_line = Line(copies, at, lambda i: rest.at[i, x], line_sem.at[2])
     rx = [Spread(copies, at, "x", lambda i, p=p: rest.at[p, i]) for p in places]
     rest_line.start()
@@ -399,28 +401,26 @@
     r0.begin(2)
     r0.parts(1)
     r0.parts(3)
-    r0.parts(0)
-    vz.end()
-    vy[2].start()
     r0.begin(1)
     r0.begin(3)
-    r0.end(2)
-    r0.begin(0)
+    r0.parts(0)
     for k in range(4):
         vy[k].end()
     swap_pred = predict(1)
+    r0.end(2)
+    r0.begin(0)
+    swap_pred.wait_recv()
+    errors(1)
+    r1.parts(2)
+    r1.begin(2)
     rest_line.arrive(0)
     rx[1].start()
     r0.end(1)
     r0.end(3)
-    swap_pred.wait_recv()
-    errors(1)
-    r1.parts(2)
-    r1.begin(2)
-    r0.z_middle()
     r1.parts(1)
     r1.parts(3)
     r1.parts(0)
+    r0.z_middle()
     r1.begin(1)
     r1.begin(3)
     r0.end(0)
@@ -449,7 +449,6 @@
     predict_rest(1)
     r1.z_end()
     fz.start()
-    fz.start_late()
     fy[0].start()
 
     def square_begin(s, total):
@@ -467,6 +466,7 @@
     sent = square_begin(0, total)
     gy[0].end()
     use(0, 0)
+    fz.start_late()
     gz.end()
     gy[2].start()
     sent = square_begin(1, square_end(0, sent))

time: 131 us -> 127 us (0.969)
  Pallas kernels: 128 us -> 124 us
    pallas_call x1, Pallas kernels: 128 us -> 124 us  [shards(): pl.pallas_call(kernel, out_shape=(jax.ShapeDtypeStruct((B, B), F32), jax....]
where the time goes in v3:
time: 127 us
  Pallas kernels  124 us (98%)
  local copies, waits for them, and re-layouts  2.36 us (2%)
    pallas_call x1, Pallas kernels, shards(): pl.pallas_call(kernel, out_shape=(jax.ShapeDtypeStruct((B, B), F32), jax....  124 us

profile of v3, /device:TPU:1, one launch (start us, length us, event | category | flops | bytes accessed | tf_op | source)
XLA Modules:
  0.0 126.5 jit_solution(6894285782333776221)
XLA Ops:
  0.6 123.5 %recalibrate.1 = (f32[256,256]{1,0:T(8,128)}, bf16[256,256]{1,0:T(8,128)(2,1)}) custom-call(s32[1,4]{1,0:T(1,128)} %counts_ref.1, bf16[256,512]{1,0:T(8,128)(2,1)} %hidden_hbm.1, bf16[256,256]{1,0:T(8,128)(2,1)} %targets_hbm.1, f32[256,256]{1,0:T(8,128)} %master_hbm.1), custom_call_target="tpu_custom_call" | custom-call | tf_op jit(solution)/shard_map/recalibrate/pallas_call | solution.py:530
  124.2 0.0 copy-start
  124.2 1.7 %copy.8 = f32[256,256]{1,0:T(8,128)} copy(f32[256,256]{1,0:T(8,128)} %get-tuple-element.4) | data formatting | bytes 524288
  125.9 0.0 copy-done
  125.9 0.7 copy.9
Async XLA Ops:
  124.2 1.7 %copy-start = (bf16[256,256]{1,0:T(8,128)(2,1)S(1)}, bf16[256,256]{1,0:T(8,128)(2,1)}, u32[]{:S(2)}) copy-start(bf16[256,256]{1,0:T(8,128)(2,1)} %get-tuple-element.5) | copy-start | bytes 393220
